TPU v7x, 32 devices: a whole 2x2x4 slice. The times are simulated.
32 devices in a mesh: dp: 16 (over z, x, core), code: 2 (over y).
Axes of the slice: x: 2, y: 2, z: 4, core: 2. Of those that a mesh axis runs over, the one named last changes fastest.
Arguments:
- items: float32 [4096, 512], P(('dp', 'code')), may hold values from -6 to 6
- codewords: float32 [8192, 512], P('code'), may hold values from -6 to 6
- assign: int32 [4096], P('dp'), may hold values from 0 to 8191, as said below
Outputs:
- new_codewords: float32 [8192, 512], P('code', 'dp')
- residual: float32 [4096, 512], P(('dp', 'code'))
Inputs may be any that keep to these rules, and one draw needn't show every extreme that they name: `assign`: the items are laid out in aligned blocks of 128 (the items of one device). Splitting the codewords into equal ranges, one per index of code, the items of one block name codewords of exactly half of the ranges, 128 items for each such range.
All inputs are finite; a program needn't handle non-finite values.
Results may differ from a plain program's by a relative error of at most 0.0003.
Values sent between devices are 32-bit elements; how exact they have to be, the bound alone decides.
A program may use at most 64 MiB of HBM per device.

v0:
```python
import jax
import jax.numpy as jnp
from jax import lax
from jax.sharding import PartitionSpec as P

K = 8192
ITERS = 3


epsilon = 1e-05
inverse_temp = 64.0


def unit_rows(values):
    return values * lax.rsqrt(jnp.mean(values * values, axis=-1, keepdims=True) + epsilon)


def kernel_of(rows_block, scaled):
    return jnp.exp(
        jnp.dot(
            unit_rows(rows_block),
            scaled.T,
            precision=lax.Precision.HIGHEST,
            preferred_element_type=jnp.float32,
        )
    )


def column_scale(col_part):
    summed = lax.psum(col_part, "dp")
    return 1.0 / (K * summed)


def row_scaling(row_part, total_items):
    summed = lax.psum(row_part, "code")
    return 1.0 / (total_items * summed)


def body(items, codewords, assign):
    code_count = lax.axis_size("code")
    dp_count = lax.axis_size("dp")
    local_codes = codewords.shape[0]
    width = items.shape[1]
    own_rows = items.shape[0]
    total_items = own_rows * code_count * dp_count
    scaled = unit_rows(codewords) * (inverse_temp / width)
    gathered = lax.all_gather(items, "code", axis=0, tiled=True)
    kernel_vals = kernel_of(gathered, scaled)
    col_part = jnp.sum(kernel_vals, axis=0)
    row_scale = jnp.ones((kernel_vals.shape[0],), jnp.float32)
    for sweep_index in range(ITERS):
        col_scale = column_scale(col_part)
        row_part = jnp.dot(
            kernel_vals,
            col_scale,
            precision=lax.Precision.HIGHEST,
            preferred_element_type=jnp.float32,
        )
        row_scale = row_scaling(row_part, total_items)
        col_part = jnp.dot(
            row_scale,
            kernel_vals,
            precision=lax.Precision.HIGHEST,
            preferred_element_type=jnp.float32,
        )
    mass = lax.psum(col_part, "dp")
    numerator = lax.dot_general(
        kernel_vals,
        row_scale[:, None] * gathered,
        (((0,), (0,)), ((), ())),
        precision=lax.Precision.HIGHEST,
        preferred_element_type=jnp.float32,
    )
    owned_sums = lax.psum_scatter(numerator, "dp", scatter_dimension=1, tiled=True)
    new_codewords = owned_sums / mass[:, None]
    my_code = lax.axis_index("code")
    offset = my_code * local_codes
    index_rows = assign - offset
    inside = (index_rows >= 0) & (index_rows < local_codes)
    picked = jnp.take(codewords, jnp.clip(index_rows, 0, local_codes - 1), axis=0)
    looked = lax.psum_scatter(
        jnp.where(inside[:, None], picked, jnp.float32(0.0)),
        "code",
        scatter_dimension=0,
        tiled=True,
    )
    residual = items - looked
    return (new_codewords, residual)


def solution(mesh):
    in_specs = (P(("dp", "code"), None), P("code", None), P("dp"))
    out_specs = (P("code", "dp"), P(("dp", "code"), None))
    return jax.shard_map(body, mesh=mesh, in_specs=in_specs, out_specs=out_specs, check_vma=False)
```

profile of v0, /device:TPU:0, one launch (start us, length us, event | category | flops | bytes accessed | tf_op | source)
XLA Modules:
  0.0 380.6 jit_solution(12260026628695852052)
XLA Ops:
  7.2 0.0 reduce-scatter.5.cloned.1.call-start
  7.2 0.7 compare_and_fusion
  7.9 4.6 %gather_fusion = f32[256,512]{1,0:T(8,128)S(1)} fusion(f32[4096,512]{1,0:T(8,128)} %param.4, s32[1024]{0:T(1024)S(1)} %pad_clamp_fusion), kind=kCustom, calls=%fused_computation | custom fusion | bytes 1049600 | tf_op jit(solution)/shard_map/jit(_take)/gather | solution.py:80
  12.5 0.9 select_select_fusion
  13.4 0.0 reduce-scatter.5.cloned.1.call-update
  13.5 0.0 copy-start.1
  13.5 0.0 reduce-scatter.3.cloned.1.call-start
  13.5 0.0 copy-start
  13.5 4.2 %multiply_reduce_fusion = f32[4096]{0:T(1024)S(1)} fusion(f32[4096,512]{1,0:T(8,128)} %param.4), kind=kLoop, calls=%fused_computation.4 | loop fusion | flops 4190208 | bytes 8404992 | tf_op jit(solution)/shard_map/reduce_sum | solution.py:15
  17.7 0.0 copy-done.1
  17.7 15.0 %all_gather.3 = f32[256,512]{1,0:T(8,128)S(1)} all-gather(f32[128,512]{1,0:T(8,128)S(1)} %copy-done.1), channel_id=1, replica_groups=mesh['dp'=16,'code'=2] {'code'}, dimensions={0}, use_global_device_ids=true | all-gather | bytes 786432 | tf_op jit(solution)/shard_map/all_gather | solution.py:47
  32.7 0.1 multiply_reduce_fusion.1
  32.8 0.0 copy-done
  32.8 9.1 %fusion.14 = (f32[4096]{0:T(1024)S(1)}, f32[256,4096]{1,0:T(8,128)}) fusion(f32[4096,512]{1,0:T(8,128)S(1)} %copy-done, f32[4096]{0:T(1024)S(1)} %add_rsqrt_fusion, f32[256,512]{1,0:T(8,128)S(1)} %all_gather.3, f32[256]{0:T(256)S(1)} %add_rsqrt_fusion.1), kind=kOutput, calls=%fused_computation.29 | convolution fusion | flops 6447820800 | bytes 13140992 | tf_op jit(solution)/shard_map/dot_general | solution.py:20
  42.0 60.0 %psum.49 = f32[4096]{0:T(1024)S(1)} all-reduce(f32[4096]{0:T(1024)S(1)} %get-tuple-element.5), channel_id=1, replica_groups=mesh['dp'=16,'code'=2] {'dp'}, use_global_device_ids=true, to_apply=%region_3.0 | all-reduce | flops 4096 | bytes 32768 | tf_op jit(solution)/shard_map/psum | solution.py:30
  101.9 5.5 %fusion.15 = f32[1,256]{1,0:T(1,128)S(1)} fusion(f32[256,4096]{1,0:T(8,128)} %get-tuple-element.6, f32[4096,1]{0,1:T(1,128)S(1)} %bitcast.25), kind=kOutput, calls=%fused_computation.30 | convolution fusion | flops 12582912 | bytes 4211712 | tf_op jit(solution)/shard_map/dot_general | solution.py:53
  107.5 5.5 %psum.50 = f32[256]{0:T(256)S(1)} all-reduce(f32[256]{0:T(256)S(1)} %bitcast.32), channel_id=1, replica_groups=mesh['dp'=16,'code'=2] {'code'}, use_global_device_ids=true, to_apply=%region_4.0 | all-reduce | flops 256 | bytes 2048 | tf_op jit(solution)/shard_map/psum | solution.py:35
  112.9 4.3 %fusion.16 = f32[1,4096]{1,0:T(1,128)S(1)} fusion(f32[256,1]{0,1:T(1,128)S(1)} %bitcast.33, f32[256,4096]{1,0:T(8,128)} %get-tuple-element.6), kind=kOutput, calls=%fused_computation.31 | convolution fusion | flops 12582912 | bytes 4211712 | tf_op jit(solution)/shard_map/dot_general | solution.py:60
  117.2 57.8 %psum.51 = f32[4096]{0:T(1024)S(1)} all-reduce(f32[4096]{0:T(1024)S(1)} %bitcast.27), channel_id=1, replica_groups=mesh['dp'=16,'code'=2] {'dp'}, use_global_device_ids=true, to_apply=%region_5.0 | all-reduce | flops 4096 | bytes 32768 | tf_op jit(solution)/shard_map/psum | solution.py:30
  175.0 5.5 %fusion.17 = f32[1,256]{1,0:T(1,128)S(1)} fusion(f32[256,4096]{1,0:T(8,128)} %get-tuple-element.6, f32[4096,1]{0,1:T(1,128)S(1)} %bitcast.28), kind=kOutput, calls=%fused_computation.32 | convolution fusion | flops 12582912 | bytes 4211712 | tf_op jit(solution)/shard_map/dot_general | solution.py:53
  180.5 4.9 %psum.52 = f32[256]{0:T(256)S(1)} all-reduce(f32[256]{0:T(256)S(1)} %bitcast.34), channel_id=1, replica_groups=mesh['dp'=16,'code'=2] {'code'}, use_global_device_ids=true, to_apply=%region_6.0 | all-reduce | flops 256 | bytes 2048 | tf_op jit(solution)/shard_map/psum | solution.py:35
  185.5 4.3 %fusion.18 = f32[1,4096]{1,0:T(1,128)S(1)} fusion(f32[256,1]{0,1:T(1,128)S(1)} %bitcast.35, f32[256,4096]{1,0:T(8,128)} %get-tuple-element.6), kind=kOutput, calls=%fused_computation.33 | convolution fusion | flops 12582912 | bytes 4211712 | tf_op jit(solution)/shard_map/dot_general | solution.py:60
  189.7 57.6 %psum.53 = f32[4096]{0:T(1024)S(1)} all-reduce(f32[4096]{0:T(1024)S(1)} %bitcast.29), channel_id=1, replica_groups=mesh['dp'=16,'code'=2] {'dp'}, use_global_device_ids=true, to_apply=%region_7.0 | all-reduce | flops 4096 | bytes 32768 | tf_op jit(solution)/shard_map/psum | solution.py:30
  247.4 5.5 %fusion.19 = f32[1,256]{1,0:T(1,128)S(1)} fusion(f32[256,4096]{1,0:T(8,128)} %get-tuple-element.6, f32[4096,1]{0,1:T(1,128)S(1)} %bitcast.30), kind=kOutput, calls=%fused_computation.34 | convolution fusion | flops 12582912 | bytes 4211712 | tf_op jit(solution)/shard_map/dot_general | solution.py:53
  252.9 5.2 %psum.54 = f32[256]{0:T(256)S(1)} all-reduce(f32[256]{0:T(256)S(1)} %bitcast.36), channel_id=1, replica_groups=mesh['dp'=16,'code'=2] {'code'}, use_global_device_ids=true, to_apply=%region_8.0 | all-reduce | flops 256 | bytes 2048 | tf_op jit(solution)/shard_map/psum | solution.py:35
  258.1 10.9 %fusion.8 = f32[4096,512]{0,1:T(8,128)} fusion(f32[256,4096]{1,0:T(8,128)} %get-tuple-element.6, f32[256,512]{1,0:T(8,128)S(1)} %all_gather.3, f32[256]{0:T(256)S(1)} %multiply_divide_fusion.3), kind=kOutput, calls=%fused_computation.9 | convolution fusion | flops 6442582016 | bytes 13108224 | tf_op jit(solution)/shard_map/dot_general | solution.py:67
  269.0 0.0 reduce-scatter.3.cloned.1.call-update
  269.0 4.3 %fusion.20 = f32[1,4096]{1,0:T(1,128)S(1)} fusion(f32[256,1]{0,1:T(1,128)S(1)} %bitcast.31, f32[256,4096]{1,0:T(8,128)} %get-tuple-element.6), kind=kOutput, calls=%fused_computation.35 | convolution fusion | flops 12582912 | bytes 4211712 | tf_op jit(solution)/shard_map/dot_general | solution.py:60
  273.3 60.4 %psum.55 = f32[4096]{0:T(1024)S(1)} all-reduce(f32[4096]{0:T(1024)S(1)} %bitcast.26), channel_id=1, replica_groups=mesh['dp'=16,'code'=2] {'dp'}, use_global_device_ids=true, to_apply=%region_10.0 | all-reduce | flops 4096 | bytes 32768 | tf_op jit(solution)/shard_map/psum | solution.py:66
  333.6 1.7 sub.11
  335.3 36.6 %reduce-scatter.3.cloned.1.call-done = f32[4096,32]{0,1:T(8,128)} async-done(((f32[4096,512]{0,1:T(8,128)}), f32[4096,32]{0,1:T(8,128)}) %reduce-scatter.3.cloned.1.call-update) | async-done | bytes 524304 | tf_op jit(solution)/shard_map/reduce_scatter | solution.py:74
  371.9 1.9 broadcast_divide_fusion
  (10 shorter events, 0.1 us)
Async XLA Ops:
  7.2 326.5 %reduce-scatter.5.cloned.1.call-start = ((), (), s32[]{:S(2)}) async-start(), calls=%async_computation.3 | async-start | bytes 786432 | tf_op jit(solution)/shard_map/reduce_scatter | solution.py:81
  13.5 4.2 %copy-start.1 = (f32[128,512]{1,0:T(8,128)S(1)}, f32[128,512]{1,0:T(8,128)}, u32[]{:S(2)}) copy-start(f32[128,512]{1,0:T(8,128)} %param.3) | copy-start | bytes 786436
  13.5 358.4 %reduce-scatter.3.cloned.1.call-start = ((), (), s32[]{:S(2)}) async-start(), calls=%async_computation.2 | async-start | bytes 8912896 | tf_op jit(solution)/shard_map/reduce_scatter | solution.py:74
  13.5 19.3 %copy-start = (f32[4096,512]{1,0:T(8,128)S(1)}, f32[4096,512]{1,0:T(8,128)}, u32[]{:S(2)}) copy-start(f32[4096,512]{1,0:T(8,128)} %param.4) | copy-start | bytes 25165828
Sparse Core Ops, SparseCore 0:
  13.6 20.7 reduce-scatter.4
  269.1 102.7 reduce-scatter.2
where the time goes:
time: 381 us
  blocking collectives  266 us (70%)
  matrix products  49.4 us (13%)
  waiting for transfers between devices  36.6 us (10%)
  between operations  14.1 us (4%)
  other arithmetic  9.53 us (3%)
  local copies, waits for them, and re-layouts  4.6 us (1%)
    psum x3, blocking collectives, column_scale(): summed = lax.psum(col_part, 'dp')  175 us
    psum x1, blocking collectives, body(): mass = lax.psum(col_part, 'dp')  60.4 us
    reduce_scatter x1, waiting for transfers between devices, body(): lax.psum_scatter(numerator, 'dp', scatter_dimension=1, tiled=True)  36.6 us
    dot_general x3, matrix products, body(): jnp.dot(kernel_vals, col_scale, precision=lax.Precision.HIGHEST, preferre...  16.6 us
    psum x3, blocking collectives, row_scaling(): summed = lax.psum(row_part, 'code')  15.6 us
    all_gather x1, blocking collectives, body(): gathered = lax.all_gather(items, 'code', axis=0, tiled=True)  15 us
    dot_general x3, matrix products, body(): jnp.dot(row_scale, kernel_vals, precision=lax.Precision.HIGHEST, preferre...  12.8 us
    dot_general x1, matrix products, body(): lax.dot_general(kernel_vals, row_scale[:, None] * gathered, (((0,), (0,))...  10.9 us
  transfers between devices with their start and end apart: 2, of which 1 were waited for; matrix products, arithmetic and copies ran while one was open for 15% of the time, Pallas kernels for 0%

commit v1 on v0

v1 whole, which is shorter than its diff:
```python
import functools

import jax
import jax.numpy as jnp
from jax import lax
from jax.experimental import pallas as pl
from jax.experimental.pallas import tpu as pltpu
from jax.sharding import PartitionSpec as P

ITERS = 3
LANES = 128
PARTS = 4
EPSILON = 1e-05
INVERSE_TEMP = 64.0
MESH = pl.DeviceIdType.MESH
F32, BF16 = jnp.float32, jnp.bfloat16


def unit_rows(values):
    return values * lax.rsqrt(jnp.mean(values * values, axis=-1, keepdims=True) + EPSILON)


def split(values):
    high = values.astype(BF16)
    return high, (values - high.astype(F32)).astype(BF16)


def dot(left, right, contract):
    return lax.dot_general(left, right, ((contract[:1], contract[1:]), ((), ())), preferred_element_type=F32)


def kernel(A, B, C, items_ref, code_ref, assign_ref, out_ref, looked_ref,
           cw, chi, clo, xs, xcat, kf, khi, klo, pick, pickr, colb, cola, rowx, rz, massb, xt, wcat,
           num, numc, numx, numr,
           load_sem, y_send, y_recv, z_send, z_recv, f_send, f_recv, p_send, p_recv,
           b_send, b_recv, a_send, a_recv, r_send, r_recv, rz_send, rz_recv, c_send, c_recv, h_send, h_recv):
    R, D = items_ref.shape
    L = code_ref.shape[0]
    G = C * R
    N = A * B
    H = B // 2
    d = D // N
    W = D // A
    TL = min(L, max(LANES, 131072 // G))
    tiles = L // TL
    Lq = L // PARTS
    dp, c = lax.axis_index("dp"), lax.axis_index("code")
    line, place = lax.div(dp, B), lax.rem(dp, B)
    outer, core = lax.div(place, 2), lax.rem(place, 2)

    def on_line(off):
        return {"dp": lax.rem(line + off, A) * B + place}

    def on_place(off):
        return {"dp": line * B + lax.rem(place + off, B)}

    def on_code(off):
        return {"code": lax.rem(c + off, C)}

    def on_outer(off):
        return {"dp": line * B + lax.rem(outer + off, H) * 2 + core}

    def remote(src, dst, send, recv, where):
        return pltpu.make_async_remote_copy(src_ref=src, dst_ref=dst, send_sem=send, recv_sem=recv,
                                            device_id=where, device_id_type=MESH)

    def start(copies):
        for copy in copies:
            copy.start()
        return copies

    def wait(copies):
        for copy in copies:
            copy.wait()

    rows = L // PARTS
    loads = [pltpu.make_async_copy(code_ref.at[pl.ds(q * rows, rows)], cw.at[pl.ds(q * rows, rows)], load_sem.at[q])
             for q in range(PARTS)]
    start(loads)
    barrier = pltpu.get_barrier_semaphore()
    peers = [on_line(o) for o in range(1, A)] + [on_place(o) for o in range(1, B)] + [on_code(o) for o in range(1, C)]
    for peer in peers:
        pl.semaphore_signal(barrier, inc=1, device_id=peer, device_id_type=MESH)
    pl.semaphore_wait(barrier, len(peers))

    y_copies = start([remote(items_ref, xs.at[0, o], y_send.at[o], y_recv.at[o], on_code(o)) for o in range(1, C)])
    z_copies = start([remote(items_ref, xs.at[o, 0], z_send.at[o], z_recv.at[o], on_line(o)) for o in range(1, A)])
    xs[0, 0] = items_ref[...]

    for q in range(PARTS):
        loads[q].wait()

        def scale(j, _):
            at = pl.ds(pl.multiple_of(q * rows + j * LANES, LANES), LANES)
            chi[at, :], clo[at, :] = split(unit_rows(cw[at, :]) * (INVERSE_TEMP / D))
            return 0
        lax.fori_loop(0, rows // LANES, scale, 0)

    def pick_for(off):
        base = lax.rem(c + off, C) * R

        def one(i, _):
            index = assign_ref[base + i] - c * L
            inside = (index >= 0) & (index < L)
            row = cw[pl.ds(jnp.clip(index, 0, L - 1), 1), :]
            pick[off, pl.ds(i, 1), :] = jnp.where(inside, row, 0.0)
            return 0
        lax.fori_loop(0, R, one, 0, unroll=8)

    for o in range(1, C):
        pick_for(o)
    p_copies = start([remote(pick.at[o], pickr.at[o], p_send.at[o], p_recv.at[o], on_code(o)) for o in range(1, C)])
    pick_for(0)

    def prepare(slot):
        for s in range(C):
            high, low = split(unit_rows(xs[slot, s]))
            xcat[s * R:(s + 1) * R, :] = high
            xcat[G + s * R:G + (s + 1) * R, :] = low
            part = xs[slot, s, :, pl.ds(pl.multiple_of(line * W, LANES), W)]
            xt[:, slot * G + s * R:slot * G + (s + 1) * R] = part.T

    def similar(slot, lo, hi, own=False):
        def step(j, _):
            at = pl.ds(pl.multiple_of(j * TL, LANES), TL)
            both = dot(xcat[...], chi[at, :], (1, 1))
            vals = jnp.exp(both[:G] + both[G:] + dot(xcat[:G, :], clo[at, :], (1, 1)))
            high, low = split(vals)
            khi[slot * G:(slot + 1) * G, at] = high
            klo[slot * G:(slot + 1) * G, at] = low
            if own:
                kf[:, at] = vals
                colb[0, 0, :, at] = jnp.sum(vals, axis=0, keepdims=True)
            return 0
        lax.fori_loop(lo, hi, step, 0)

    wait(y_copies)
    prepare(0)
    similar(0, 0, tiles, True)

    def start_b(t):
        return start([remote(colb.at[t, 0], colb.at[t, o], b_send.at[t, o], b_recv.at[t, o], on_place(o))
                      for o in range(1, B)])

    def start_a(t):
        total = colb[t, 0]
        for o in range(1, B):
            total = total + colb[t, o]
        cola[t, 0] = total
        return start([remote(cola.at[t, 0], cola.at[t, o], a_send.at[t, o], a_recv.at[t, o], on_line(o))
                      for o in range(1, A)])

    def column_total(t):
        total = cola[t, 0]
        for o in range(1, A):
            total = total + cola[t, o]
        return total

    forwards = {}

    def forward(o):
        z_copies[o - 1].wait()
        forwards[o] = start([remote(xs.at[o, 0], xs.at[o, s], f_send.at[o, s], f_recv.at[o, s], on_code(s))
                             for s in range(1, C)])

    def begin_block(o, lo, hi):
        if lo == 0:
            wait(forwards[o])
            prepare(o)
        similar(o, lo, hi)

    half = tiles // 2
    work = [[lambda o=o: forward(o)] for o in range(1, A)]
    for o in range(1, A):
        work.append([lambda o=o: begin_block(o, 0, half)])
        work.append([lambda o=o: begin_block(o, half, tiles)])

    def background():
        if work:
            for job in work.pop(0):
                job()

    for t in range(ITERS):
        copies = start_b(t)
        background()
        wait(copies)
        copies = start_a(t)
        background()
        wait(copies)
        massb[...] = 1.0 / (C * L * column_total(t))

        def row_step(j, acc):
            at = pl.ds(pl.multiple_of(j * LANES, LANES), LANES)
            return acc + kf[:, at] * massb[:, at]
        acc = lax.fori_loop(0, L // LANES, row_step, jnp.zeros((G, LANES), F32), unroll=4)
        rowx[t, 0] = jnp.sum(acc.T, axis=0, keepdims=True)
        copies = start([remote(rowx.at[t, 0], rowx.at[t, o], r_send.at[t, o], r_recv.at[t, o], on_code(o))
                        for o in range(1, C)])
        background()
        wait(copies)
        total = rowx[t, 0]
        for o in range(1, C):
            came = rowx[t, o]
            total = total + jnp.concatenate([came[:, G - o * R:], came[:, :G - o * R]], axis=1)
        row_scale = 1.0 / (N * G * total)
        if t == ITERS - 1:
            rz[0] = row_scale
            rz_copies = start([remote(rz.at[0], rz.at[o], rz_send.at[o], rz_recv.at[o], on_line(o))
                               for o in range(1, A)])
        spread = jnp.broadcast_to(row_scale, (LANES, G)).T

        def col_step(j, _):
            at = pl.ds(pl.multiple_of(j * LANES, LANES), LANES)
            colb[t + 1, 0, :, at] = jnp.sum(kf[:, at] * spread, axis=0, keepdims=True)
            return 0
        lax.fori_loop(0, L // LANES, col_step, 0, unroll=4)

    copies = start_b(ITERS)
    while work:
        background()
    wait(rz_copies)
    for o in range(A):
        high, low = split(xt[:, o * G:(o + 1) * G] * rz[o])
        wcat[:W, o * G:(o + 1) * G] = high
        wcat[W:, o * G:(o + 1) * G] = low

    def weighted(q):
        def step(j, _):
            TN = min(Lq, 512)
            src = pl.ds(pl.multiple_of(q * Lq + j * TN, LANES), TN)
            dst = pl.ds(pl.multiple_of(j * TN, LANES), TN)
            both = dot(wcat[...], khi[:, src], (1, 0))
            vals = both[:W] + both[W:] + dot(wcat[:W, :], klo[:, src], (1, 0))
            for g in range(B):
                num[q, g % 2, g // 2, :, dst] = vals[g * d:(g + 1) * d]
            return 0
        lax.fori_loop(0, Lq // min(Lq, 512), step, 0)
        return start([remote(num.at[q, 1 - core], numc.at[q], c_send.at[q], c_recv.at[q],
                             {"dp": line * B + outer * 2 + (1 - core)})])

    def exchange(q):
        numx[q] = num[q, core] + numc[q]
        return start([remote(numx.at[q, lax.rem(outer + o, H)], numr.at[q, o], h_send.at[q, o], h_recv.at[q, o],
                             on_outer(o)) for o in range(1, H)])

    core_copies, outer_copies = [], []
    for q in range(PARTS):
        core_copies.append(weighted(q))
        if q == 0:
            wait(copies)
            copies = start_a(ITERS)
        else:
            wait(core_copies[q - 1])
            outer_copies.append(exchange(q - 1))
    wait(core_copies[PARTS - 1])
    outer_copies.append(exchange(PARTS - 1))
    wait(p_copies)
    looked = pick[0]
    for o in range(1, C):
        looked = looked + pickr[o]
    looked_ref[...] = looked
    wait(copies)
    massb[...] = 1.0 / column_total(ITERS)
    for q in range(PARTS):
        wait(outer_copies[q])
        total = numx[q, outer]
        for o in range(1, H):
            total = total + numr[q, o]
        out_ref[:, q * Lq:(q + 1) * Lq] = total * massb[:, q * Lq:(q + 1) * Lq]


def body(items, codewords, assign):
    C, N = lax.axis_size("code"), lax.axis_size("dp")
    R, D = items.shape
    L = codewords.shape[0]
    A = D // LANES
    B, G, d, H, Lq = N // A, C * R, D // N, N // A // 2, L // PARTS
    dma = pltpu.SemaphoreType.DMA
    T = ITERS + 1
    flops = 2 * 3 * A * G * L * (D + LANES)
    out, looked = pl.pallas_call(
        functools.partial(kernel, A, B, C),
        out_shape=(jax.ShapeDtypeStruct((d, L), F32), jax.ShapeDtypeStruct((R, D), F32)),
        in_specs=[pl.BlockSpec(memory_space=pltpu.VMEM), pl.BlockSpec(memory_space=pl.ANY),
                  pl.BlockSpec(memory_space=pltpu.SMEM)],
        out_specs=[pl.BlockSpec(memory_space=pltpu.VMEM)] * 2,
        scratch_shapes=[
            pltpu.VMEM((L, D), F32), pltpu.VMEM((L, D), BF16), pltpu.VMEM((L, D), BF16),
            pltpu.VMEM((A, C, R, D), F32), pltpu.VMEM((2 * G, D), BF16),
            pltpu.VMEM((G, L), F32), pltpu.VMEM((A * G, L), BF16), pltpu.VMEM((A * G, L), BF16),
            pltpu.VMEM((C, R, D), F32), pltpu.VMEM((C, R, D), F32),
            pltpu.VMEM((T, B, 1, L), F32), pltpu.VMEM((T, A, 1, L), F32),
            pltpu.VMEM((ITERS, C, 1, G), F32), pltpu.VMEM((A, 1, G), F32), pltpu.VMEM((1, L), F32),
            pltpu.VMEM((D // A, A * G), F32), pltpu.VMEM((2 * (D // A), A * G), BF16),
            pltpu.VMEM((PARTS, 2, H, d, Lq), F32), pltpu.VMEM((PARTS, H, d, Lq), F32),
            pltpu.VMEM((PARTS, H, d, Lq), F32), pltpu.VMEM((PARTS, H, d, Lq), F32),
            dma((PARTS,)), dma((C,)), dma((C,)), dma((A,)), dma((A,)), dma((A, C)), dma((A, C)), dma((C,)), dma((C,)),
            dma((T, B)), dma((T, B)), dma((T, A)), dma((T, A)), dma((ITERS, C)), dma((ITERS, C)),
            dma((A,)), dma((A,)), dma((PARTS,)), dma((PARTS,)), dma((PARTS, H)), dma((PARTS, H)),
        ],
        compiler_params=pltpu.CompilerParams(collective_id=0, has_side_effects=True,
                                             vmem_limit_bytes=60 * 1024 * 1024),
        cost_estimate=pl.CostEstimate(flops=flops, bytes_accessed=4 * (L * D + 4 * R * D), transcendentals=A * G * L),
        name="sinkhorn_level",
    )(items, codewords, assign)
    return out.T, items - looked


def solution(mesh):
    in_specs = (P(("dp", "code"), None), P("code", None), P("dp"))
    out_specs = (P("code", "dp"), P(("dp", "code"), None))
    return jax.shard_map(body, mesh=mesh, in_specs=in_specs, out_specs=out_specs, check_vma=False)
```

time: 381 us -> 88 us (0.23)
  blocking collectives: 266 us -> 0 us
  Pallas kernels: 0 us -> 83.5 us
  matrix products: 49.4 us -> 0 us
  waiting for transfers between devices: 36.6 us -> 0 us
  between operations: 14.1 us -> 0.65 us
  other arithmetic: 9.53 us -> 1.69 us
    psum x7 -> x0, blocking collectives: 251 us -> none  [the longest x3 175 us: column_scale(): summed = lax.psum(col_part, 'dp')]
    pallas_call x0 -> x1, Pallas kernels: none -> 83.5 us  [body(): pl.pallas_call(functools.partial(kernel, A, B, C), out_shape=(jax.ShapeDt...]
    dot_general x8 -> x0, matrix products: 49.4 us -> none  [the longest x3 16.6 us: body(): jnp.dot(kernel_vals, col_scale, precision=lax.Precision.HIGHEST, preferre...]
    reduce_scatter x2 -> x0, waiting for transfers between devices: 36.6 us -> none  [the longest x1 36.6 us: body(): lax.psum_scatter(numerator, 'dp', scatter_dimension=1, tiled=True)]
    all_gather x1 -> x0, blocking collectives: 15 us -> none  [body(): gathered = lax.all_gather(items, 'code', axis=0, tiled=True)]
    gather x1 -> x0, local copies, waits for them, and re-layouts: 4.59 us -> none  [body(): jnp.take(codewords, jnp.clip(index_rows, 0, local_codes - 1), axis=0)]
    reduce_sum x2 -> x0, other arithmetic: 4.28 us -> none  [unit_rows(): jnp.mean(values * values, axis=-1, keepdims=True) + epsilon]
  transfers between devices with their start and end apart: 2 -> 0, of which waited for: 1 -> 0; matrix products, arithmetic and copies ran while one was open for 15% -> 0% of each run, Pallas kernels for 0% -> 0%
where the time goes in v1:
time: 88 us; the launch traced here: 87.8 us
  Pallas kernels  83.5 us (95%)
  local copies, waits for them, and re-layouts  1.87 us (2%)
  other arithmetic  1.69 us (2%)
    pallas_call x1, Pallas kernels, body(): pl.pallas_call(functools.partial(kernel, A, B, C), out_shape=(jax.ShapeDt...  83.5 us
    unnamed x3, local copies, waits for them, and re-layouts  1.87 us

profile of v1, /device:TPU:0, one launch (start us, length us, event | category | flops | bytes accessed | tf_op | source)
XLA Modules:
  0.0 87.8 jit_solution(10985274156467507280)
XLA Ops:
  0.6 0.0 copy-start
  0.6 83.5 %sinkhorn_level.1 = (f32[32,4096]{1,0:T(8,128)}, f32[128,512]{1,0:T(8,128)}) custom-call(f32[128,512]{1,0:T(8,128)} %items_ref.1, f32[4096,512]{1,0:T(8,128)} %code_ref.1, s32[256]{0:T(256)} %assign_ref.1), custom_call_target="tpu_custom_call" | custom-call | flops 16106127360 | bytes 9437184 | tf_op jit(solution)/shard_map/sinkhorn_level/pallas_call | solution.py:281
  84.2 0.0 copy-done
  84.2 1.7 %sub.3 = f32[128,512]{1,0:T(8,128)} subtract(f32[128,512]{1,0:T(8,128)S(1)} %copy-done, f32[128,512]{1,0:T(8,128)} %get-tuple-element.5) | non-fusion elementwise | flops 65536 | bytes 786432 | tf_op jit(solution)/shard_map/sub | solution.py:306
  85.9 1.9 %copy.6 = f32[4096,32]{0,1:T(8,128)} copy(f32[4096,32]{0,1:T(8,128)} %bitcast.1) | data formatting | bytes 1048576
Async XLA Ops:
  0.6 83.6 %copy-start = (f32[128,512]{1,0:T(8,128)S(1)}, f32[128,512]{1,0:T(8,128)}, u32[]{:S(2)}) copy-start(f32[128,512]{1,0:T(8,128)} %items_ref.1) | copy-start | bytes 786436

commit v2 on v1

--- a/solution.py
+++ b/solution.py
@@ -84,7 +84,9 @@
     pl.semaphore_wait(barrier, len(peers))
 
     y_copies = start([remote(items_ref, xs.at[0, o], y_send.at[o], y_recv.at[o], on_code(o)) for o in range(1, C)])
-    z_copies = start([remote(items_ref, xs.at[o, 0], z_send.at[o], z_recv.at[o], on_line(o)) for o in range(1, A)])
+    near = sorted(range(1, A), key=lambda o: min(o, A - o))
+    z_copies = {o: remote(items_ref, xs.at[o, 0], z_send.at[o], z_recv.at[o], on_line(o)) for o in near}
+    start([z_copies[o] for o in near[:2]])
     xs[0, 0] = items_ref[...]
 
     for q in range(PARTS):
@@ -107,10 +109,7 @@
             return 0
         lax.fori_loop(0, R, one, 0, unroll=8)
 
-    for o in range(1, C):
-        pick_for(o)
-    p_copies = start([remote(pick.at[o], pickr.at[o], p_send.at[o], p_recv.at[o], on_code(o)) for o in range(1, C)])
-    pick_for(0)
+    p_copies = [remote(pick.at[o], pickr.at[o], p_send.at[o], p_recv.at[o], on_code(o)) for o in range(1, C)]
 
     def prepare(slot):
         for s in range(C):
@@ -159,7 +158,7 @@
     forwards = {}
 
     def forward(o):
-        z_copies[o - 1].wait()
+        z_copies[o].wait()
         forwards[o] = start([remote(xs.at[o, 0], xs.at[o, s], f_send.at[o, s], f_recv.at[o, s], on_code(s))
                              for s in range(1, C)])
 
@@ -170,10 +169,16 @@
         similar(o, lo, hi)
 
     half = tiles // 2
-    work = [[lambda o=o: forward(o)] for o in range(1, A)]
-    for o in range(1, A):
+    def pick_all():
+        for o in range(C):
+            pick_for(o)
+
+    work = [[lambda: forward(near[0]), lambda: start([z_copies[o] for o in near[2:]])], [pick_all],
+            [lambda: forward(near[1])]]
+    for o in near:
         work.append([lambda o=o: begin_block(o, 0, half)])
         work.append([lambda o=o: begin_block(o, half, tiles)])
+    work[3] = [lambda o=o: forward(o) for o in near[2:]] + [lambda: start(p_copies)] + work[3]
 
     def background():
         if work:
@@ -267,6 +272,11 @@
         for o in range(1, H):
             total = total + numr[q, o]
         out_ref[:, q * Lq:(q + 1) * Lq] = total * massb[:, q * Lq:(q + 1) * Lq]
+
+
+def finish(total_ref, items_ref, looked_ref, out_ref, residual_ref):
+    out_ref[...] = total_ref[...]
+    residual_ref[...] = items_ref[...] - looked_ref[...]
 
 
 def body(items, codewords, assign):
@@ -303,7 +313,14 @@
         cost_estimate=pl.CostEstimate(flops=flops, bytes_accessed=4 * (L * D + 4 * R * D), transcendentals=A * G * L),
         name="sinkhorn_level",
     )(items, codewords, assign)
-    return out.T, items - looked
+    new_codewords, residual = pl.pallas_call(
+        finish,
+        out_shape=(jax.ShapeDtypeStruct((d, L), F32), jax.ShapeDtypeStruct((R, D), F32)),
+        in_specs=[pl.BlockSpec(memory_space=pltpu.VMEM)] * 3,
+        out_specs=[pl.BlockSpec(memory_space=pltpu.VMEM)] * 2,
+        name="write_outputs",
+    )(out, items, looked)
+    return new_codewords.T, residual
 
 
 def solution(mesh):

time: 88 us -> 87 us (0.989)
  Pallas kernels: 83.5 us -> 86.2 us
  local copies, waits for them, and re-layouts: 1.87 us -> 0 us
  other arithmetic: 1.69 us -> 0 us
    pallas_call x0 -> x1, Pallas kernels: none -> 2.1 us  [body(): pl.pallas_call(finish, out_shape=(jax.ShapeDtypeStruct((d, L), F32), jax....]
    unnamed x3 -> x0, local copies, waits for them, and re-layouts: 1.87 us -> none
    sub x1 -> x0, other arithmetic: 1.69 us -> none  [body(): return (out.T, items - looked)]
where the time goes in v2:
time: 87 us; the launch traced here: 86.9 us
  Pallas kernels  86.2 us (99%)
    pallas_call x1, Pallas kernels, body(): pl.pallas_call(functools.partial(kernel, A, B, C), out_shape=(jax.ShapeDt...  84.1 us
    pallas_call x1, Pallas kernels, body(): pl.pallas_call(finish, out_shape=(jax.ShapeDtypeStruct((d, L), F32), jax....  2.1 us

profile of v2, /device:TPU:0, one launch (start us, length us, event | category | flops | bytes accessed | tf_op | source)
XLA Modules:
  0.0 86.9 jit_solution(6883985536947694589)
XLA Ops:
  0.6 84.1 %sinkhorn_level.1 = (f32[32,4096]{1,0:T(8,128)}, f32[128,512]{1,0:T(8,128)}) custom-call(f32[128,512]{1,0:T(8,128)} %items_ref.3, f32[4096,512]{1,0:T(8,128)} %code_ref.1, s32[256]{0:T(256)} %assign_ref.1), custom_call_target="tpu_custom_call" | custom-call | flops 16106127360 | bytes 9437184 | tf_op jit(solution)/shard_map/sinkhorn_level/pallas_call | solution.py:291
  84.8 2.1 %write_outputs.1 = (f32[32,4096]{1,0:T(8,128)}, f32[128,512]{1,0:T(8,128)}) custom-call(f32[32,4096]{1,0:T(8,128)} %get-tuple-element.6.total_ref, f32[128,512]{1,0:T(8,128)} %items_ref.3, f32[128,512]{1,0:T(8,128)} %get-tuple-element.7.looked_ref), custom_call_target="tpu_custom_call" | custom-call | tf_op jit(solution)/shard_map/write_outputs/pallas_call | solution.py:316

commit v3 on v2

--- a/solution.py
+++ b/solution.py
@@ -30,7 +30,7 @@
 
 
 def kernel(A, B, C, items_ref, code_ref, assign_ref, out_ref, looked_ref,
-           cw, chi, clo, xs, xcat, kf, khi, klo, pick, pickr, colb, cola, rowx, rz, massb, xt, wcat,
+           cw, ccat, xs, xcat, kf, khi, klo, pick, pickr, colb, cola, rowx, rz, massb, xt, wcat,
            num, numc, numx, numr,
            load_sem, y_send, y_recv, z_send, z_recv, f_send, f_recv, p_send, p_recv,
            b_send, b_recv, a_send, a_recv, r_send, r_recv, rz_send, rz_recv, c_send, c_recv, h_send, h_recv):
@@ -41,7 +41,7 @@
     H = B // 2
     d = D // N
     W = D // A
-    TL = min(L, max(LANES, 131072 // G))
+    TL = min(L, max(LANES, 65536 // G))
     tiles = L // TL
     Lq = L // PARTS
     dp, c = lax.axis_index("dp"), lax.axis_index("code")
@@ -94,7 +94,10 @@
 
         def scale(j, _):
             at = pl.ds(pl.multiple_of(q * rows + j * LANES, LANES), LANES)
-            chi[at, :], clo[at, :] = split(unit_rows(cw[at, :]) * (INVERSE_TEMP / D))
+            high, low = split(unit_rows(cw[at, :]) * (INVERSE_TEMP / D))
+            ccat[at, :D] = high
+            ccat[at, D:2 * D] = high
+            ccat[at, 2 * D:] = low
             return 0
         lax.fori_loop(0, rows // LANES, scale, 0)
 
@@ -114,16 +117,16 @@
     def prepare(slot):
         for s in range(C):
             high, low = split(unit_rows(xs[slot, s]))
-            xcat[s * R:(s + 1) * R, :] = high
-            xcat[G + s * R:G + (s + 1) * R, :] = low
+            xcat[s * R:(s + 1) * R, :D] = high
+            xcat[s * R:(s + 1) * R, D:2 * D] = low
+            xcat[s * R:(s + 1) * R, 2 * D:] = high
             part = xs[slot, s, :, pl.ds(pl.multiple_of(line * W, LANES), W)]
             xt[:, slot * G + s * R:slot * G + (s + 1) * R] = part.T
 
     def similar(slot, lo, hi, own=False):
         def step(j, _):
             at = pl.ds(pl.multiple_of(j * TL, LANES), TL)
-            both = dot(xcat[...], chi[at, :], (1, 1))
-            vals = jnp.exp(both[:G] + both[G:] + dot(xcat[:G, :], clo[at, :], (1, 1)))
+            vals = jnp.exp(dot(xcat[...], ccat[at, :], (1, 1)))
             high, low = split(vals)
             khi[slot * G:(slot + 1) * G, at] = high
             klo[slot * G:(slot + 1) * G, at] = low
@@ -131,7 +134,7 @@
                 kf[:, at] = vals
                 colb[0, 0, :, at] = jnp.sum(vals, axis=0, keepdims=True)
             return 0
-        lax.fori_loop(lo, hi, step, 0)
+        lax.fori_loop(lo, hi, step, 0, unroll=4)
 
     wait(y_copies)
     prepare(0)
@@ -295,8 +298,8 @@
                   pl.BlockSpec(memory_space=pltpu.SMEM)],
         out_specs=[pl.BlockSpec(memory_space=pltpu.VMEM)] * 2,
         scratch_shapes=[
-            pltpu.VMEM((L, D), F32), pltpu.VMEM((L, D), BF16), pltpu.VMEM((L, D), BF16),
-            pltpu.VMEM((A, C, R, D), F32), pltpu.VMEM((2 * G, D), BF16),
+            pltpu.VMEM((L, D), F32), pltpu.VMEM((L, 3 * D), BF16),
+            pltpu.VMEM((A, C, R, D), F32), pltpu.VMEM((G, 3 * D), BF16),
             pltpu.VMEM((G, L), F32), pltpu.VMEM((A * G, L), BF16), pltpu.VMEM((A * G, L), BF16),
             pltpu.VMEM((C, R, D), F32), pltpu.VMEM((C, R, D), F32),
             pltpu.VMEM((T, B, 1, L), F32), pltpu.VMEM((T, A, 1, L), F32),

time: 87 us -> 86.4 us (level)
  no operation moved by 1% of the time
where the time goes in v3:
time: 86.4 us; the launch traced here: 86.2 us
  Pallas kernels  85.6 us (99%)
    pallas_call x1, Pallas kernels, body(): pl.pallas_call(functools.partial(kernel, A, B, C), out_shape=(jax.ShapeDt...  83.5 us
    pallas_call x1, Pallas kernels, body(): pl.pallas_call(finish, out_shape=(jax.ShapeDtypeStruct((d, L), F32), jax....  2.1 us

profile of v3, /device:TPU:0, one launch (start us, length us, event | category | flops | bytes accessed | tf_op | source)
XLA Modules:
  0.0 86.2 jit_solution(5083410872525481896)
XLA Ops:
  0.6 83.5 %sinkhorn_level.1 = (f32[32,4096]{1,0:T(8,128)}, f32[128,512]{1,0:T(8,128)}) custom-call(f32[128,512]{1,0:T(8,128)} %items_ref.3, f32[4096,512]{1,0:T(8,128)} %code_ref.1, s32[256]{0:T(256)} %assign_ref.1), custom_call_target="tpu_custom_call" | custom-call | flops 16106127360 | bytes 9437184 | tf_op jit(solution)/shard_map/sinkhorn_level/pallas_call | solution.py:294
  84.1 2.1 %write_outputs.1 = (f32[32,4096]{1,0:T(8,128)}, f32[128,512]{1,0:T(8,128)}) custom-call(f32[32,4096]{1,0:T(8,128)} %get-tuple-element.6.total_ref, f32[128,512]{1,0:T(8,128)} %items_ref.3, f32[128,512]{1,0:T(8,128)} %get-tuple-element.7.looked_ref), custom_call_target="tpu_custom_call" | custom-call | tf_op jit(solution)/shard_map/write_outputs/pallas_call | solution.py:319

commit v4 on v3

--- a/solution.py
+++ b/solution.py
@@ -94,10 +94,12 @@
 
         def scale(j, _):
             at = pl.ds(pl.multiple_of(q * rows + j * LANES, LANES), LANES)
-            high, low = split(unit_rows(cw[at, :]) * (INVERSE_TEMP / D))
-            ccat[at, :D] = high
-            ccat[at, D:2 * D] = high
-            ccat[at, 2 * D:] = low
+            codes = cw[at, :].T
+            norm = lax.rsqrt(jnp.mean(codes * codes, axis=0, keepdims=True) + EPSILON) * (INVERSE_TEMP / D)
+            high, low = split(codes * norm)
+            ccat[:D, at] = high
+            ccat[D:2 * D, at] = high
+            ccat[2 * D:, at] = low
             return 0
         lax.fori_loop(0, rows // LANES, scale, 0)
 
@@ -126,7 +128,7 @@
     def similar(slot, lo, hi, own=False):
         def step(j, _):
             at = pl.ds(pl.multiple_of(j * TL, LANES), TL)
-            vals = jnp.exp(dot(xcat[...], ccat[at, :], (1, 1)))
+            vals = jnp.exp(dot(xcat[...], ccat[:, at], (1, 0)))
             high, low = split(vals)
             khi[slot * G:(slot + 1) * G, at] = high
             klo[slot * G:(slot + 1) * G, at] = low
@@ -176,12 +178,17 @@
         for o in range(C):
             pick_for(o)
 
-    work = [[lambda: forward(near[0]), lambda: start([z_copies[o] for o in near[2:]])], [pick_all],
-            [lambda: forward(near[1])]]
-    for o in near:
-        work.append([lambda o=o: begin_block(o, 0, half)])
-        work.append([lambda o=o: begin_block(o, half, tiles)])
-    work[3] = [lambda o=o: forward(o) for o in near[2:]] + [lambda: start(p_copies)] + work[3]
+    def start_far():
+        start([z_copies[o] for o in near[2:]])
+
+    def forward_far():
+        for o in near[2:]:
+            forward(o)
+        start(p_copies)
+
+    halves = [(lambda o=o, lo=lo: begin_block(o, lo, lo + half)) for o in near for lo in (0, half)]
+    work = [[start_far, pick_all], [lambda: forward(near[0])], [lambda: forward(near[1])], halves[0:1], halves[1:2],
+            [forward_far] + halves[2:3], halves[3:4], [], halves[4:5], halves[5:]]
 
     def background():
         if work:
@@ -298,7 +305,7 @@
                   pl.BlockSpec(memory_space=pltpu.SMEM)],
         out_specs=[pl.BlockSpec(memory_space=pltpu.VMEM)] * 2,
         scratch_shapes=[
-            pltpu.VMEM((L, D), F32), pltpu.VMEM((L, 3 * D), BF16),
+            pltpu.VMEM((L, D), F32), pltpu.VMEM((3 * D, L), BF16),
             pltpu.VMEM((A, C, R, D), F32), pltpu.VMEM((G, 3 * D), BF16),
             pltpu.VMEM((G, L), F32), pltpu.VMEM((A * G, L), BF16), pltpu.VMEM((A * G, L), BF16),
             pltpu.VMEM((C, R, D), F32), pltpu.VMEM((C, R, D), F32),

time: 86.4 us -> 85.9 us (level)
  no operation moved by 1% of the time
where the time goes in v4:
time: 85.9 us; the launch traced here: 85.7 us
  Pallas kernels  85.1 us (99%)
    pallas_call x1, Pallas kernels, body(): pl.pallas_call(functools.partial(kernel, A, B, C), out_shape=(jax.ShapeDt...  83 us
    pallas_call x1, Pallas kernels, body(): pl.pallas_call(finish, out_shape=(jax.ShapeDtypeStruct((d, L), F32), jax....  2.1 us

profile of v4, /device:TPU:0, one launch (start us, length us, event | category | flops | bytes accessed | tf_op | source)
XLA Modules:
  0.0 85.7 jit_solution(3773500789388568653)
XLA Ops:
  0.6 83.0 %sinkhorn_level.1 = (f32[32,4096]{1,0:T(8,128)}, f32[128,512]{1,0:T(8,128)}) custom-call(f32[128,512]{1,0:T(8,128)} %items_ref.3, f32[4096,512]{1,0:T(8,128)} %code_ref.1, s32[256]{0:T(256)} %assign_ref.1), custom_call_target="tpu_custom_call" | custom-call | flops 16106127360 | bytes 9437184 | tf_op jit(solution)/shard_map/sinkhorn_level/pallas_call | solution.py:301
  83.6 2.1 %write_outputs.1 = (f32[32,4096]{1,0:T(8,128)}, f32[128,512]{1,0:T(8,128)}) custom-call(f32[32,4096]{1,0:T(8,128)} %get-tuple-element.6.total_ref, f32[128,512]{1,0:T(8,128)} %items_ref.3, f32[128,512]{1,0:T(8,128)} %get-tuple-element.7.looked_ref), custom_call_target="tpu_custom_call" | custom-call | tf_op jit(solution)/shard_map/write_outputs/pallas_call | solution.py:326

commit v5 on v4

--- a/solution.py
+++ b/solution.py
@@ -178,17 +178,9 @@
         for o in range(C):
             pick_for(o)
 
-    def start_far():
-        start([z_copies[o] for o in near[2:]])
-
-    def forward_far():
-        for o in near[2:]:
-            forward(o)
-        start(p_copies)
-
     halves = [(lambda o=o, lo=lo: begin_block(o, lo, lo + half)) for o in near for lo in (0, half)]
-    work = [[start_far, pick_all], [lambda: forward(near[0])], [lambda: forward(near[1])], halves[0:1], halves[1:2],
-            [forward_far] + halves[2:3], halves[3:4], [], halves[4:5], halves[5:]]
+    work = [[lambda: pick_for(0)], [lambda: [pick_for(o) for o in range(1, C)]], [],
+            [], halves[0:1], halves[1:2], halves[2:3], halves[3:4], halves[4:5], halves[5:]]
 
     def background():
         if work:
@@ -202,6 +194,8 @@
         copies = start_a(t)
         background()
         wait(copies)
+        if t == 0:
+            start([z_copies[o] for o in near[2:]])
         massb[...] = 1.0 / (C * L * column_total(t))
 
         def row_step(j, acc):
@@ -213,6 +207,10 @@
                         for o in range(1, C)])
         background()
         wait(copies)
+        for o in (near[:2], near[2:], ())[t]:
+            forward(o)
+        if t == ITERS - 1:
+            start(p_copies)
         total = rowx[t, 0]
         for o in range(1, C):
             came = rowx[t, o]

time: 85.9 us -> 81.2 us (0.945)
  Pallas kernels: 85.1 us -> 80.4 us
    pallas_call x1, Pallas kernels: 83 us -> 78.3 us  [body(): pl.pallas_call(functools.partial(kernel, A, B, C), out_shape=(jax.ShapeDt...]
where the time goes in v5:
time: 81.2 us; the launch traced here: 81 us
  Pallas kernels  80.4 us (99%)
    pallas_call x1, Pallas kernels, body(): pl.pallas_call(functools.partial(kernel, A, B, C), out_shape=(jax.ShapeDt...  78.3 us
    pallas_call x1, Pallas kernels, body(): pl.pallas_call(finish, out_shape=(jax.ShapeDtypeStruct((d, L), F32), jax....  2.1 us

profile of v5, /device:TPU:0, one launch (start us, length us, event | category | flops | bytes accessed | tf_op | source)
XLA Modules:
  0.0 81.0 jit_solution(16153799794266697613)
XLA Ops:
  0.6 78.3 %sinkhorn_level.1 = (f32[32,4096]{1,0:T(8,128)}, f32[128,512]{1,0:T(8,128)}) custom-call(f32[128,512]{1,0:T(8,128)} %items_ref.3, f32[4096,512]{1,0:T(8,128)} %code_ref.1, s32[256]{0:T(256)} %assign_ref.1), custom_call_target="tpu_custom_call" | custom-call | flops 16106127360 | bytes 9437184 | tf_op jit(solution)/shard_map/sinkhorn_level/pallas_call | solution.py:299
  78.9 2.1 %write_outputs.1 = (f32[32,4096]{1,0:T(8,128)}, f32[128,512]{1,0:T(8,128)}) custom-call(f32[32,4096]{1,0:T(8,128)} %get-tuple-element.6.total_ref, f32[128,512]{1,0:T(8,128)} %items_ref.3, f32[128,512]{1,0:T(8,128)} %get-tuple-element.7.looked_ref), custom_call_target="tpu_custom_call" | custom-call | tf_op jit(solution)/shard_map/write_outputs/pallas_call | solution.py:324

commit v6 on v5

--- a/solution.py
+++ b/solution.py
@@ -9,7 +9,7 @@
 
 ITERS = 3
 LANES = 128
-PARTS = 4
+PARTS = 8
 EPSILON = 1e-05
 INVERSE_TEMP = 64.0
 MESH = pl.DeviceIdType.MESH
@@ -86,7 +86,7 @@
     y_copies = start([remote(items_ref, xs.at[0, o], y_send.at[o], y_recv.at[o], on_code(o)) for o in range(1, C)])
     near = sorted(range(1, A), key=lambda o: min(o, A - o))
     z_copies = {o: remote(items_ref, xs.at[o, 0], z_send.at[o], z_recv.at[o], on_line(o)) for o in near}
-    start([z_copies[o] for o in near[:2]])
+    start([z_copies[near[0]]])
     xs[0, 0] = items_ref[...]
 
     for q in range(PARTS):
@@ -102,6 +102,8 @@
             ccat[2 * D:, at] = low
             return 0
         lax.fori_loop(0, rows // LANES, scale, 0)
+
+    start([z_copies[o] for o in near[1:2]])
 
     def pick_for(off):
         base = lax.rem(c + off, C) * R
@@ -138,7 +140,15 @@
             return 0
         lax.fori_loop(lo, hi, step, 0, unroll=4)
 
+    forwards = {}
+
+    def forward(o):
+        z_copies[o].wait()
+        forwards[o] = start([remote(xs.at[o, 0], xs.at[o, s], f_send.at[o, s], f_recv.at[o, s], on_code(s))
+                             for s in range(1, C)])
+
     wait(y_copies)
+    forward(near[0])
     prepare(0)
     similar(0, 0, tiles, True)
 
@@ -160,13 +170,6 @@
             total = total + cola[t, o]
         return total
 
-    forwards = {}
-
-    def forward(o):
-        z_copies[o].wait()
-        forwards[o] = start([remote(xs.at[o, 0], xs.at[o, s], f_send.at[o, s], f_recv.at[o, s], on_code(s))
-                             for s in range(1, C)])
-
     def begin_block(o, lo, hi):
         if lo == 0:
             wait(forwards[o])
@@ -174,13 +177,9 @@
         similar(o, lo, hi)
 
     half = tiles // 2
-    def pick_all():
-        for o in range(C):
-            pick_for(o)
-
     halves = [(lambda o=o, lo=lo: begin_block(o, lo, lo + half)) for o in near for lo in (0, half)]
-    work = [[lambda: pick_for(0)], [lambda: [pick_for(o) for o in range(1, C)]], [],
-            [], halves[0:1], halves[1:2], halves[2:3], halves[3:4], halves[4:5], halves[5:]]
+    work = [[lambda: pick_for(0)], [lambda: [pick_for(o) for o in range(1, C)]], halves[0:1],
+            halves[1:2], halves[2:3], halves[3:4], [], halves[4:5], halves[5:], []]
 
     def background():
         if work:
@@ -189,6 +188,9 @@
 
     for t in range(ITERS):
         copies = start_b(t)
+        if t == 0:
+            for o in near[1:2]:
+                forward(o)
         background()
         wait(copies)
         copies = start_a(t)
@@ -207,8 +209,9 @@
                         for o in range(1, C)])
         background()
         wait(copies)
-        for o in (near[:2], near[2:], ())[t]:
-            forward(o)
+        if t == 1:
+            for o in near[2:]:
+                forward(o)
         if t == ITERS - 1:
             start(p_copies)
         total = rowx[t, 0]

time: 81.2 us -> 81.6 us (level)
  no operation moved by 1% of the time
where the time goes in v6:
time: 81.6 us; the launch traced here: 81.4 us
  Pallas kernels  80.8 us (99%)
    pallas_call x1, Pallas kernels, body(): pl.pallas_call(functools.partial(kernel, A, B, C), out_shape=(jax.ShapeDt...  78.7 us
    pallas_call x1, Pallas kernels, body(): pl.pallas_call(finish, out_shape=(jax.ShapeDtypeStruct((d, L), F32), jax....  2.1 us

profile of v6, /device:TPU:0, one launch (start us, length us, event | category | flops | bytes accessed | tf_op | source)
XLA Modules:
  0.0 81.4 jit_solution(5790989771661112361)
XLA Ops:
  0.6 78.7 %sinkhorn_level.1 = (f32[32,4096]{1,0:T(8,128)}, f32[128,512]{1,0:T(8,128)}) custom-call(f32[128,512]{1,0:T(8,128)} %items_ref.3, f32[4096,512]{1,0:T(8,128)} %code_ref.1, s32[256]{0:T(256)} %assign_ref.1), custom_call_target="tpu_custom_call" | custom-call | flops 16106127360 | bytes 9437184 | tf_op jit(solution)/shard_map/sinkhorn_level/pallas_call | solution.py:302
  79.3 2.1 %write_outputs.1 = (f32[32,4096]{1,0:T(8,128)}, f32[128,512]{1,0:T(8,128)}) custom-call(f32[32,4096]{1,0:T(8,128)} %get-tuple-element.6.total_ref, f32[128,512]{1,0:T(8,128)} %items_ref.3, f32[128,512]{1,0:T(8,128)} %get-tuple-element.7.looked_ref), custom_call_target="tpu_custom_call" | custom-call | tf_op jit(solution)/shard_map/write_outputs/pallas_call | solution.py:327
